TPU v7x, 128 devices: a whole 4x4x4 slice. The times are simulated.
128 devices in a mesh: seq: 16 (over z, y), expert: 8 (over x, core).
Axes of the slice: x: 4, y: 4, z: 4, core: 2. Of those that a mesh axis runs over, the one named last changes fastest.
Arguments:
- tokens: bfloat16 [2048, 4096], P(('seq', 'expert')), may hold values from -6 to 6
- gain_mamba: float32 [4096], replicated, may hold values from 0.1 to 1.9
- in_weight: bfloat16 [2, 4096, 8192], P(None, 'seq', 'expert'), may hold values from -0.09375 to 0.09375
- conv_weight: float32 [4, 8192], P(None, 'expert'), may hold values from -3 to 3
- conv_bias: float32 [8192], P('expert'), may hold values from -3 to 3
- xproj_weight: bfloat16 [8192, 288], P('expert'), may hold values from -0.0625 to 0.0625
- dt_weight: bfloat16 [256, 8192], P(None, 'expert'), may hold values from -0.375 to 0.375
- dt_bias: float32 [8192], P('expert'), may hold values from -7 to -2
- a_rate: float32 [16, 8192], P(None, 'expert'), may hold values from 0.01 to 8
- skip_d: float32 [8192], P('expert'), may hold values from 0.5 to 1.5
- out_weight: bfloat16 [8192, 4096], P('expert', 'seq'), may hold values from -0.0625 to 0.0625
- gain_moe: float32 [4096], replicated, may hold values from 0.1 to 1.9
- expert_ids: int32 [2048, 2], P(('seq', 'expert')), may hold values from 0 to 15, all different within a row; in each aligned block of 16 rows (0 to 15, 16 to 31, ...) at most 4 rows name the same one
- gate_weights: float32 [2048, 2], P(('seq', 'expert')), may hold values from 0.2 to 1
- w_gate: bfloat16 [16, 4096, 7168], P('seq', None, 'expert'), may hold values from -0.09375 to 0.09375
- w_up: bfloat16 [16, 4096, 7168], P('seq', None, 'expert'), may hold values from -0.09375 to 0.09375
- w_down: bfloat16 [16, 7168, 4096], P('seq', 'expert'), may hold values from -0.0625 to 0.0625
Outputs:
- mixed: bfloat16 [2048, 4096], P(('seq', 'expert'))
Inputs may be any that keep to these rules, and one draw needn't show every extreme that they name: `expert_ids`: each row names 2 different experts. In each aligned block of 16 rows (the rows of one device) no expert is named by more than 4 rows, a bound that some block reaches.
All inputs are finite; a program needn't handle non-finite values.
Results may differ from a plain program's by a relative error of at most 0.03.
Values may be sent and summed in bfloat16 or wider, within the bound.
A program may use at most 192 MiB of HBM per device.

v0:
```python
import jax
import jax.numpy as jnp
from jax import lax
from jax.sharding import PartitionSpec as P

STATE = 16
CONV = 4
RANK = 256
TOP = 2


def from_behind(block, axis, distance):
    devices = range(lax.axis_size(axis))
    route = [(i - distance, i) for i in devices if i - distance in devices]
    return lax.ppermute(block, axis, route)


def rms_norm(values, gain):
    wide = values.astype(jnp.float32)
    return wide * lax.rsqrt(jnp.mean(wide * wide, axis=-1, keepdims=True) + 1e-05) * gain


def combine_states(earlier, later):
    return (earlier[0] * later[0], later[0] * earlier[1] + later[1])


def per_device(
    tokens,
    gain_mamba,
    in_weight,
    conv_weight,
    conv_bias,
    xproj_weight,
    dt_weight,
    dt_bias,
    a_rate,
    skip_d,
    out_weight,
    gain_moe,
    expert_ids,
    gate_weights,
    w_gate,
    w_up,
    w_down,
):
    rows, dim = tokens.shape
    n_seq = lax.axis_size("seq")
    n_exp = lax.axis_size("expert")
    group = lax.all_gather(tokens, "expert", axis=0, tiled=True)
    local_tok = group.shape[0]
    normed = rms_norm(group, gain_mamba).astype(jnp.bfloat16)
    both = jnp.einsum(
        "td,kdc->tkc",
        normed,
        lax.all_gather(in_weight, "seq", axis=1, tiled=True),
        preferred_element_type=jnp.float32,
    )
    xpart = both[:, 0]
    zpart = both[:, 1]
    edge = from_behind(xpart[local_tok - (CONV - 1) :], "seq", 1)
    padded = jnp.concatenate([edge, xpart], axis=0)
    conv = conv_bias
    for tap in range(CONV):
        conv = conv + conv_weight[tap] * padded[tap : tap + local_tok]
    inner = jax.nn.silu(conv).astype(jnp.bfloat16)
    partial_value = jnp.dot(inner, xproj_weight, preferred_element_type=jnp.float32)
    low_part, edge_part = (
        lax.psum(partial_value[:, :RANK].astype(jnp.bfloat16), "expert").astype(jnp.float32),
        lax.psum(partial_value[:, RANK:].astype(jnp.bfloat16), "expert").astype(jnp.float32),
    )
    dt_low = low_part.astype(jnp.bfloat16)
    bmat = edge_part[:, :STATE]
    cmat = edge_part[:, STATE:]
    step = jax.nn.softplus(jnp.dot(dt_low, dt_weight, preferred_element_type=jnp.float32) + dt_bias)
    inner_f = inner.astype(jnp.float32)
    decay = jnp.exp(-step[:, None, :] * a_rate[None, :, :])
    source = bmat[:, :, None] * (step * inner_f)[:, None, :]
    cumulative, states = lax.associative_scan(combine_states, (decay, source), axis=0)
    total = cumulative[-1]
    final = states[-1]

    def relay(turn, incoming):
        return from_behind((total * incoming + final).astype(jnp.bfloat16), "seq", 1).astype(
            jnp.float32
        )

    arriving = lax.fori_loop(0, n_seq - 1, relay, jnp.zeros_like(final))
    states = states + cumulative * arriving[None, :, :]
    readout = jnp.sum(cmat[:, :, None] * states, axis=1)
    gated = ((readout + skip_d * inner_f) * jax.nn.silu(zpart)).astype(jnp.bfloat16)
    terms = jnp.dot(
        gated,
        lax.all_gather(out_weight, "seq", axis=1, tiled=True),
        preferred_element_type=jnp.float32,
    )
    mixer = lax.psum_scatter(
        terms.astype(jnp.bfloat16), "expert", scatter_dimension=0, tiled=True
    ).astype(jnp.float32)
    resid = (tokens.astype(jnp.float32) + mixer).astype(jnp.bfloat16)
    normed2 = rms_norm(resid, gain_moe).astype(jnp.bfloat16)
    capacity = max(2, 4 * rows // n_seq)
    slots_all = n_seq * capacity
    flat_ids = expert_ids.reshape(-1)
    order = jnp.arange(flat_ids.shape[0], dtype=jnp.int32)
    same = (flat_ids[:, None] == flat_ids[None, :]) & (order[None, :] < order[:, None])
    slot = jnp.sum(same.astype(jnp.int32), axis=1)
    target = flat_ids * capacity + slot
    places = target[:, None] == jnp.arange(slots_all, dtype=jnp.int32)[None, :]
    dispatch_mat = jnp.any(places.reshape(rows, TOP, slots_all), axis=1).astype(jnp.bfloat16)
    send = jnp.einsum(
        "rp,rd->pd", dispatch_mat, normed2, preferred_element_type=jnp.float32
    ).astype(jnp.bfloat16)
    received = lax.all_to_all(
        send.reshape(n_seq, capacity, dim), "seq", split_axis=0, concat_axis=0, tiled=True
    )
    pooled = lax.all_gather(
        received.reshape(1, slots_all, dim), "expert", axis=0, tiled=True
    ).reshape(n_exp * slots_all, dim)
    gate = jnp.dot(pooled, w_gate[0], preferred_element_type=jnp.float32)
    upper = jnp.dot(pooled, w_up[0], preferred_element_type=jnp.float32)
    act = (jax.nn.silu(gate) * upper).astype(jnp.bfloat16)
    outputs = lax.psum_scatter(
        jnp.dot(act, w_down[0], preferred_element_type=jnp.float32).astype(jnp.bfloat16),
        "expert",
        scatter_dimension=0,
        tiled=True,
    )
    returned = lax.all_to_all(
        outputs.reshape(n_seq, capacity, dim), "seq", split_axis=0, concat_axis=0, tiled=True
    ).reshape(slots_all, dim)
    weighting = jnp.where(places, gate_weights.reshape(-1)[:, None], 0.0)
    weighting = jnp.sum(weighting.reshape(rows, TOP, slots_all), axis=1)
    moe = jnp.dot(weighting, returned.astype(jnp.float32), precision=lax.Precision.HIGHEST)
    return (resid.astype(jnp.float32) + moe).astype(jnp.bfloat16)


def solution(mesh):
    placed = (
        P(("seq", "expert"), None),
        P(),
        P(None, "seq", "expert"),
        P(None, "expert"),
        P("expert"),
        P("expert", None),
        P(None, "expert"),
        P("expert"),
        P(None, "expert"),
        P("expert"),
        P("expert", "seq"),
        P(),
        P(("seq", "expert"), None),
        P(("seq", "expert"), None),
        P("seq", None, "expert"),
        P("seq", None, "expert"),
        P("seq", "expert", None),
    )
    return jax.shard_map(
        per_device,
        mesh=mesh,
        in_specs=placed,
        out_specs=P(("seq", "expert"), None),
        check_vma=False,
    )
```

profile of v0, /device:TPU:0, one launch (start us, length us, event | category | flops | bytes accessed | tf_op | source)
XLA Modules:
  0.0 910.1 jit_solution(3287583702979538523)
XLA Ops:
  8.9 26.0 %all-gather.5.cloned.1.call-done = bf16[128,4096]{1,0:T(8,128)(2,1)} async-done(((bf16[16,4096]{1,0:T(8,128)(2,1)}), bf16[128,4096]{1,0:T(8,128)(2,1)}) %all-gather.5.cloned.1.call-update) | async-done | bytes 1048592 | tf_op jit(solution)/shard_map/all_gather | solution.py:49
  36.5 111.9 %all-gather.7.cloned.1.call-done = bf16[2,4096,1024]{2,1,0:T(8,128)(2,1)} async-done(((bf16[2,256,1024]{2,1,0:T(8,128)(2,1)}), bf16[2,4096,1024]{2,1,0:T(8,128)(2,1)}) %all-gather.7.cloned.1.call-update) | async-done | bytes 16777232 | tf_op jit(solution)/shard_map/all_gather | solution.py:55
  148.4 8.5 fusion.20
  163.9 14.0 %psum.14 = bf16[128,32]{0,1:T(8,128)(2,1)S(1)} all-reduce(bf16[128,32]{0,1:T(8,128)(2,1)S(1)} %slice.341), channel_id=1, replica_groups=mesh['seq'=16,'expert'=8] {'expert'}, use_global_device_ids=true, to_apply=%region_1.2 | all-reduce | flops 4096 | bytes 16384 | tf_op jit(solution)/shard_map/psum | solution.py:69
  178.7 44.8 %all-reduce.30.cloned.1.call-done = bf16[128,256]{0,1:T(8,128)(2,1)} async-done(((bf16[128,256]{0,1:T(8,128)(2,1)}), bf16[128,256]{0,1:T(8,128)(2,1)}) %all-reduce.30.cloned.1.call-update) | async-done | bytes 65552 | tf_op jit(solution)/shard_map/psum | solution.py:68
  233.5 10.9 %slice_add_fusion = (f32[64,16,1024]{2,1,0:T(8,128)S(1)}, f32[64,16,1024]{2,1,0:T(8,128)}) fusion(f32[128,16,1024]{2,1,0:T(8,128)} %copy-done.3, f32[128,16,1024]{2,1,0:T(8,128)} %copy-done.2), kind=kLoop, calls=%fused_computation.19 | loop fusion | flops 3145728 | bytes 25165824 | tf_op jit(solution)/shard_map/add | solution.py:24
  308.6 7.0 pad.108
  315.6 10.2 %pad.109 = f32[32,16,1024]{2,1,0:T(8,128)} pad(f32[16,16,1024]{2,1,0:T(8,128)} %add.263, f32[]{:T(128)} %constant.11.clone.1), padding=1_0_1x0_0_0x0_0_0 | pad | bytes 3145732 | tf_op jit(solution)/shard_map/pad | solution.py:78
  325.8 10.1 %pad.95 = f32[32,16,1024]{2,1,0:T(8,128)} pad(f32[16,16,1024]{2,1,0:T(8,128)} %add.253, f32[]{:T(128)} %constant.11.clone.1), padding=1_0_1x0_0_0x0_0_0 | pad | bytes 3145732 | tf_op jit(solution)/shard_map/pad | solution.py:78
  338.2 10.2 %pad.94 = f32[32,16,1024]{2,1,0:T(8,128)} pad(f32[16,16,1024]{2,1,0:T(8,128)} %pad_maximum_fusion.4, f32[]{:T(128)} %constant.11.clone.1), padding=0_1_1x0_0_0x0_0_0 | pad | bytes 3145732 | tf_op jit(solution)/shard_map/pad | solution.py:78
  348.4 4.3 add.255
  355.7 5.0 fusion.16
  362.3 18.7 %pad.96 = f32[64,16,1024]{2,1,0:T(8,128)} pad(f32[32,16,1024]{2,1,0:T(8,128)} %pad_maximum_fusion.2, f32[]{:T(128)} %constant.11.clone.1), padding=0_1_1x0_0_0x0_0_0 | pad | bytes 6291460 | tf_op jit(solution)/shard_map/pad | solution.py:78
  381.0 12.1 %pad.97 = f32[64,16,1024]{2,1,0:T(8,128)} pad(f32[32,16,1024]{2,1,0:T(8,128)S(1)} %copy-done.16, f32[]{:T(128)} %constant.11.clone.1), padding=1_0_1x0_0_0x0_0_0 | pad | bytes 6291460 | tf_op jit(solution)/shard_map/pad | solution.py:78
  393.1 6.9 add.257
  400.0 35.8 %pad.99 = f32[128,16,1024]{2,1,0:T(8,128)} pad(f32[64,16,1024]{2,1,0:T(8,128)} %add.257, f32[]{:T(128)} %constant.11.clone.1), padding=1_0_1x0_0_0x0_0_0 | pad | bytes 12582916 | tf_op jit(solution)/shard_map/pad | solution.py:78
  437.2 18.7 %pad.110 = f32[64,16,1024]{2,1,0:T(8,128)} pad(f32[32,16,1024]{2,1,0:T(8,128)} %pad_maximum_fusion.3, f32[]{:T(128)} %constant.11.clone.1), padding=0_1_1x0_0_0x0_0_0 | pad | bytes 6291460 | tf_op jit(solution)/shard_map/pad | solution.py:78
  455.9 12.1 %pad.111 = f32[64,16,1024]{2,1,0:T(8,128)} pad(f32[32,16,1024]{2,1,0:T(8,128)S(1)} %copy-done.15, f32[]{:T(128)} %constant.11.clone.1), padding=1_0_1x0_0_0x0_0_0 | pad | bytes 6291460 | tf_op jit(solution)/shard_map/pad | solution.py:78
  468.0 7.1 add.265
  476.6 7.6 fusion.12
  486.7 35.8 %pad.98 = f32[128,16,1024]{2,1,0:T(8,128)} pad(f32[64,16,1024]{2,1,0:T(8,128)} %pad_maximum_fusion, f32[]{:T(128)} %constant.11.clone.1), padding=0_1_1x0_0_0x0_0_0 | pad | bytes 12582916 | tf_op jit(solution)/shard_map/pad | solution.py:78
  522.5 35.7 %pad.113 = f32[128,16,1024]{2,1,0:T(8,128)} pad(f32[64,16,1024]{2,1,0:T(8,128)} %add.265, f32[]{:T(128)} %constant.11.clone.1), padding=1_0_1x0_0_0x0_0_0 | pad | bytes 12582916 | tf_op jit(solution)/shard_map/pad | solution.py:78
  558.2 4.8 pad_maximum_fusion.1
  563.0 35.6 %pad.112 = f32[128,16,1024]{2,1,0:T(8,128)} pad(f32[64,16,1024]{2,1,0:T(8,128)} %pad_maximum_fusion.1, f32[]{:T(128)} %constant.11.clone.1), padding=0_1_1x0_0_0x0_0_0 | pad | bytes 12582916 | tf_op jit(solution)/shard_map/pad | solution.py:78
  600.4 107.7 %while.11 = (s32[]{:T(128)}, f32[16,1024]{1,0:T(8,128)S(1)}, f32[16,1024]{1,0:T(8,128)S(1)}, f32[16,1024]{1,0:T(8,128)S(1)}, s32[]{:T(128)}, /*index=5*/s32[]{:T(128)}) while((s32[]{:T(128)}, f32[16,1024]{1,0:T(8,128)S(1)}, f32[16,1024]{1,0:T(8,128)S(1)}, f32[16,1024]{1,0:T(8,128)S(1)}, s32[]{:T(128)}, /*index=5*/s32[]{:T(128)}) %tuple.47), condition=%wide.region_4.5_spmd.clone, body=%wide.region_3.4_spmd.clone.sunk | while | flops 81923 | bytes 458871 | solution.py:87
  605.5 4.2 collective-permute-start
  611.3 4.3 collective-permute-start
  617.3 4.2 collective-permute-start
  628.9 5.6 collective-permute-start
  636.1 6.5 collective-permute-start
  644.2 6.5 collective-permute-start
  652.3 6.3 collective-permute-start
  660.3 6.3 collective-permute-start
  668.2 6.3 collective-permute-start
  676.3 6.2 collective-permute-start
  684.1 6.3 collective-permute-start
  692.1 6.5 collective-permute-start
  700.2 6.3 collective-permute-start
  708.1 14.0 %multiply_reduce_fusion = f32[128,1024]{1,0:T(8,128)S(1)} fusion(f32[128,16,1024]{2,1,0:T(8,128)} %pad.112, f32[128,16,1024]{2,1,0:T(8,128)} %pad.113, f32[128,16,1024]{2,1,0:T(8,128)} %pad.98, f32[128,16,1024]{2,1,0:T(8,128)} %pad.99, f32[16,1024]{1,0:T(8,128)S(1)} %get-tuple-element.27, f32[128,16]{1,0:T(8,128)S(1)} %copy-done.28), kind=kLoop, calls=%fused_computation.3 | loop fusion | flops 12451840 | bytes 34152448 | tf_op jit(solution)/shard_map/reduce_sum | solution.py:89
  722.2 5.7 convolution_convert_fusion
  728.6 39.9 %reduce-scatter.3.cloned.1.call-done = bf16[16,4096]{1,0:T(8,128)(2,1)} async-done(((bf16[128,4096]{1,0:T(8,128)(2,1)}), bf16[16,4096]{1,0:T(8,128)(2,1)}) %reduce-scatter.3.cloned.1.call-update) | async-done | bytes 131088 | tf_op jit(solution)/shard_map/reduce_scatter | solution.py:96
  771.0 16.8 %all_to_all.10 = bf16[16,4,4096]{2,1,0:T(4,128)(2,1)S(1)} all-to-all(bf16[16,4,4096]{2,1,0:T(4,128)(2,1)S(1)} %reshape.79), channel_id=1, replica_groups=mesh['seq'=16,'expert'=8] {'seq'}, dimensions={0} | all-to-all | bytes 1048576 | tf_op jit(solution)/shard_map/all_to_all | solution.py:113
  788.8 29.3 %all-gather.11.cloned.1.call-done = bf16[8,64,4096]{2,1,0:T(8,128)(2,1)} async-done(((bf16[1,64,4096]{2,1,0:T(8,128)(2,1)}), bf16[8,64,4096]{2,1,0:T(8,128)(2,1)}) %all-gather.11.cloned.1.call-update) | async-done | bytes 4194320 | tf_op jit(solution)/shard_map/all_gather | solution.py:116
  818.1 10.1 %fusion.6 = f32[512,896]{1,0:T(8,128)} fusion(bf16[512,4096]{1,0:T(8,128)(2,1)} %bitcast.51, bf16[1,4096,896]{2,1,0:T(8,128)(2,1)} %param.33), kind=kOutput, calls=%fused_computation.9 | convolution fusion | flops 3758096384 | bytes 13369344 | tf_op jit(solution)/shard_map/dot_general | solution.py:119
  828.2 16.6 %fusion.8 = bf16[512,4096]{1,0:T(8,128)(2,1)} fusion(bf16[1,896,4096]{2,1,0:T(8,128)(2,1)} %param.35, f32[512,896]{1,0:T(8,128)} %fusion.6, bf16[512,4096]{1,0:T(8,128)(2,1)} %bitcast.52, bf16[1,4096,896]{2,1,0:T(8,128)(2,1)} %param.34), kind=kOutput, calls=%fused_computation.11 | convolution fusion | flops 7521042432 | bytes 24903680 | tf_op jit(solution)/shard_map/dot_general | solution.py:123
  844.9 38.0 %reduce-scatter.5.cloned.1.call-done = bf16[64,4096]{1,0:T(8,128)(2,1)} async-done(((bf16[512,4096]{1,0:T(8,128)(2,1)}), bf16[64,4096]{1,0:T(8,128)(2,1)}) %reduce-scatter.5.cloned.1.call-update) | async-done | bytes 524304 | tf_op jit(solution)/shard_map/reduce_scatter | solution.py:122
  885.0 7.0 all-to-all-start.1
  892.1 10.1 %all-to-all-done.1 = bf16[16,4,4096]{2,1,0:T(4,128)(2,1)S(1)} async-done(((bf16[16,4,4096]{2,1,0:T(4,128)(2,1)}), bf16[16,4,4096]{2,1,0:T(4,128)(2,1)S(1)}, u32[]{:S(2)}, u32[]{:S(2)}) %all-to-all-start.1) | async-done | bytes 524320 | tf_op jit(solution)/shard_map/all_to_all | solution.py:128
  (239 shorter events, 139.0 us)
Async XLA Ops:
  6.5 155.7 %copy-start = (bf16[1024,288]{0,1:T(8,128)(2,1)S(1)}, bf16[1024,288]{0,1:T(8,128)(2,1)}, u32[]{:S(2)}) copy-start(bf16[1024,288]{0,1:T(8,128)(2,1)} %param.24) | copy-start | bytes 1769476
  6.5 28.4 %all-gather.5.cloned.1.call-start = ((), (), s32[]{:S(2)}) async-start(), calls=%async_computation.4 | async-start | bytes 1179648 | tf_op jit(solution)/shard_map/all_gather | solution.py:49
  7.3 141.1 %all-gather.7.cloned.1.call-start = ((), (), s32[]{:S(2)}) async-start(), calls=%async_computation.5 | async-start | bytes 17825792 | tf_op jit(solution)/shard_map/all_gather | solution.py:55
  8.0 215.6 %all-reduce.30.cloned.1.call-start = ((), (), s32[]{:S(2)}) async-start(), calls=%async_computation.6 | async-start | bytes 131072 | tf_op jit(solution)/shard_map/psum | solution.py:68
  36.4 125.5 %copy-start.39 = (f32[1024]{0:T(1024)S(1)}, f32[1024]{0:T(1024)}, u32[]{:S(2)}) copy-start(f32[1024]{0:T(1024)} %param.23) | copy-start | bytes 12292
  36.4 187.1 %copy-start.42 = (bf16[256,1024]{1,0:T(8,128)(2,1)S(1)}, bf16[256,1024]{1,0:T(8,128)(2,1)}, u32[]{:S(2)}) copy-start(bf16[256,1024]{1,0:T(8,128)(2,1)} %param.25) | copy-start | bytes 1572868
  36.4 187.1 %copy-start.43 = (f32[1024]{0:T(1024)S(1)}, f32[1024]{0:T(1024)}, u32[]{:S(2)}) copy-start(f32[1024]{0:T(1024)} %param.26) | copy-start | bytes 12292
  156.9 68.0 %copy-start.37 = (f32[16,1024]{1,0:T(8,128)S(1)}, f32[16,1024]{1,0:T(8,128)}, u32[]{:S(2)}) copy-start(f32[16,1024]{1,0:T(8,128)} %param.27) | copy-start | bytes 196612
  156.9 5.0 collective-permute-start.1
  162.2 64.8 %copy-start.23 = (bf16[128,1024]{1,0:T(8,128)(2,1)}, bf16[128,1024]{1,0:T(8,128)(2,1)S(1)}, u32[]{:S(2)}) copy-start(bf16[128,1024]{1,0:T(8,128)(2,1)S(1)} %multiply_convert_fusion.1) | copy-start | bytes 786436
  163.2 558.9 %all-gather.9.cloned.1.call-start = ((), (), s32[]{:S(2)}) async-start(), calls=%async_computation.7 | async-start | bytes 8912896 | tf_op jit(solution)/shard_map/all_gather | solution.py:93
  163.8 604.6 %reduce-scatter.3.cloned.1.call-start = ((), (), s32[]{:S(2)}) async-start(), calls=%async_computation.8 | async-start | bytes 1179648 | tf_op jit(solution)/shard_map/reduce_scatter | solution.py:96
  280.4 8.3 copy-start.36
  288.7 8.3 copy-start.20
  308.6 27.3 %copy-start.33 = (f32[1,16,1024]{2,1,0:T(8,128)S(1)}, f32[1,16,1024]{2,1,0:T(8,128)}, u32[]{:S(2)}) copy-start(f32[1,16,1024]{2,1,0:T(8,128)} %slice.347) | copy-start | bytes 196612
  362.3 18.7 %copy-start.16 = (f32[32,16,1024]{2,1,0:T(8,128)S(1)}, f32[32,16,1024]{2,1,0:T(8,128)}, u32[]{:S(2)}) copy-start(f32[32,16,1024]{2,1,0:T(8,128)} %add.255) | copy-start | bytes 6291460
  400.0 35.8 %copy-start.17 = (f32[31,16,1024]{2,1,0:T(8,128)S(1)}, f32[31,16,1024]{2,1,0:T(8,128)}, u32[]{:S(2)}) copy-start(f32[31,16,1024]{2,1,0:T(8,128)} %get-tuple-element.56) | copy-start | bytes 6094852
  400.0 35.8 %copy-start.31 = (f32[1,16,1024]{2,1,0:T(8,128)S(1)}, f32[1,16,1024]{2,1,0:T(8,128)}, u32[]{:S(2)}) copy-start(f32[1,16,1024]{2,1,0:T(8,128)} %slice.369) | copy-start | bytes 196612
  437.2 18.7 %copy-start.15 = (f32[32,16,1024]{2,1,0:T(8,128)S(1)}, f32[32,16,1024]{2,1,0:T(8,128)}, u32[]{:S(2)}) copy-start(f32[32,16,1024]{2,1,0:T(8,128)} %add.264) | copy-start | bytes 6291460
  468.0 8.6 copy-start.6
  522.5 35.8 %copy-start.29 = (f32[1,16,1024]{2,1,0:T(8,128)S(1)}, f32[1,16,1024]{2,1,0:T(8,128)}, u32[]{:S(2)}) copy-start(f32[1,16,1024]{2,1,0:T(8,128)} %slice.368) | copy-start | bytes 196612
  563.0 145.1 %copy-start.28 = (f32[128,16]{1,0:T(8,128)S(1)}, f32[128,16]{1,0:T(8,128)}, u32[]{:S(2)}) copy-start(f32[128,16]{1,0:T(8,128)} %copy.42) | copy-start | bytes 24580
  600.5 5.0 collective-permute-start
  605.5 5.8 collective-permute-start
  611.3 5.9 collective-permute-start
  617.3 5.8 collective-permute-start
  623.1 5.8 collective-permute-start
  628.9 7.2 collective-permute-start
  636.1 8.1 collective-permute-start
  644.2 8.1 collective-permute-start
  652.3 7.9 collective-permute-start
  660.3 7.9 collective-permute-start
  668.2 8.0 collective-permute-start
  676.3 7.8 collective-permute-start
  684.1 7.9 collective-permute-start
  692.1 8.1 collective-permute-start
  700.2 7.9 collective-permute-start
  708.1 14.1 %copy-start.19 = (f32[128,2,1024]{2,0,1:T(8,128)S(1)}, f32[128,2,1024]{2,0,1:T(8,128)}, u32[]{:S(2)}) copy-start(f32[128,2,1024]{2,0,1:T(8,128)} %copy-done.18) | copy-start | bytes 3145732
  708.1 14.1 %copy-start.24 = (bf16[128,1024]{1,0:T(8,128)(2,1)S(1)}, bf16[128,1024]{1,0:T(8,128)(2,1)}, u32[]{:S(2)}) copy-start(bf16[128,1024]{1,0:T(8,128)(2,1)} %copy-done.23) | copy-start | bytes 786436
  708.1 14.1 %copy-start.44 = (f32[1024]{0:T(1024)S(1)}, f32[1024]{0:T(1024)}, u32[]{:S(2)}) copy-start(f32[1024]{0:T(1024)} %param.28) | copy-start | bytes 12292
  722.1 46.4 %copy-start.21 = (bf16[16,4096]{1,0:T(8,128)(2,1)S(1)}, bf16[16,4096]{1,0:T(8,128)(2,1)}, u32[]{:S(2)}) copy-start(bf16[16,4096]{1,0:T(8,128)(2,1)} %param.19) | copy-start | bytes 393220
  722.1 47.4 %copy-start.38 = (f32[4096]{0:T(1024)S(1)}, f32[4096]{0:T(1024)}, u32[]{:S(2)}) copy-start(f32[4096]{0:T(1024)} %param.30) | copy-start | bytes 49156
  727.9 90.2 %all-gather.11.cloned.1.call-start = ((), (), s32[]{:S(2)}) async-start(), calls=%async_computation.9 | async-start | bytes 4718592 | tf_op jit(solution)/shard_map/all_gather | solution.py:116
  788.8 94.2 %reduce-scatter.5.cloned.1.call-start = ((), (), s32[]{:S(2)}) async-start(), calls=%async_computation.10 | async-start | bytes 4718592 | tf_op jit(solution)/shard_map/reduce_scatter | solution.py:122
  828.2 75.1 %copy-start.1 = (bf16[1024,288]{0,1:T(8,128)(2,1)S(1)}, bf16[1024,288]{0,1:T(8,128)(2,1)}, u32[]{:S(2)}) copy-start(bf16[1024,288]{0,1:T(8,128)(2,1)} %param.24) | copy-start | bytes 1769476
  844.9 47.2 %copy-start.41 = (f32[16,2]{0,1:T(2,128)S(1)}, f32[16,2]{0,1:T(2,128)}, u32[]{:S(2)}) copy-start(f32[16,2]{0,1:T(2,128)} %param.32) | copy-start | bytes 388
  844.9 57.4 %copy-start.22 = (bf16[16,4096]{1,0:T(8,128)(2,1)S(1)}, bf16[16,4096]{1,0:T(8,128)(2,1)}, u32[]{:S(2)}) copy-start(bf16[16,4096]{1,0:T(8,128)(2,1)} %reduce-scatter.3.cloned.1.call-done) | copy-start | bytes 393220
  885.0 17.2 %all-to-all-start.1 = ((bf16[16,4,4096]{2,1,0:T(4,128)(2,1)}), bf16[16,4,4096]{2,1,0:T(4,128)(2,1)S(1)}, u32[]{:S(2)}, u32[]{:S(2)}) async-start(bf16[16,4,4096]{2,1,0:T(4,128)(2,1)} %reshape.82), calls=%async_computation.3 | async-start | bytes 1048576 | tf_op jit(solution)/shard_map/all_to_all | solution.py:128
  (21 other events, 86.8 us)
Sparse Core Ops, SparseCore 0:
  9.1 25.7 all-gather.4
  37.0 111.3 all-gather.6
  163.4 60.1 all-reduce.29
  225.7 77.5 all-gather.8
  728.0 40.3 reduce-scatter.2
  788.9 29.2 all-gather.10
  845.0 37.8 reduce-scatter.4
where the time goes:
time: 926 us; the launch traced here: 910 us
  waiting for transfers between devices  327 us (35%)
  local copies, waits for them, and re-layouts  290 us (31%)
  other arithmetic  109 us (12%)
  starting transfers between devices  94.1 us (10%)
  matrix products  44.8 us (5%)
  blocking collectives  30.8 us (3%)
  between operations  14 us (2%)
    pad x24, local copies, waits for them, and re-layouts, per_device(): lax.associative_scan(combine_states, (decay, source), axis=0)  268 us
    all_gather x1, waiting for transfers between devices, per_device(): lax.all_gather(in_weight, 'seq', axis=1, tiled=True)  112 us
    ppermute x16, starting transfers between devices, from_behind(): return lax.ppermute(block, axis, route)  86.9 us
    psum x1, waiting for transfers between devices, per_device(): lax.psum(partial_value[:, :RANK].astype(jnp.bfloat16), 'expert')  44.8 us
    reduce_scatter x1, waiting for transfers between devices, per_device(): lax.psum_scatter(terms.astype(jnp.bfloat16), 'expert', scatter_dimension=...  39.9 us
    reduce_scatter x1, waiting for transfers between devices, per_device(): lax.psum_scatter(jnp.dot(act, w_down[0], preferred_element_type=jnp.float...  38 us
    add x12, other arithmetic, combine_states(): return (earlier[0] * later[0], later[0] * earlier[1] + later[1])  34.6 us
    add x12, other arithmetic, per_device(): lax.associative_scan(combine_states, (decay, source), axis=0)  33.2 us
  transfers between devices with their start and end apart: 24, of which 23 were waited for; matrix products, arithmetic and copies ran while one was open for 43% of the time, Pallas kernels for 0%

commit v1 on v0

--- a/solution.py
+++ b/solution.py
@@ -7,6 +7,14 @@
 CONV = 4
 RANK = 256
 TOP = 2
+
+
+def gather_by_exchange(array, axis, dim):
+    length = lax.axis_size(axis)
+    repeats = [length if d == dim else 1 for d in range(array.ndim)]
+    return lax.all_to_all(
+        jnp.tile(array, repeats), axis, split_axis=dim, concat_axis=dim, tiled=True
+    )
 
 
 def from_behind(block, axis, distance):
@@ -52,7 +60,7 @@
     both = jnp.einsum(
         "td,kdc->tkc",
         normed,
-        lax.all_gather(in_weight, "seq", axis=1, tiled=True),
+        gather_by_exchange(in_weight, "seq", 1),
         preferred_element_type=jnp.float32,
     )
     xpart = both[:, 0]

time: 926 us -> 1070 us (1.16)
  waiting for transfers between devices: 327 us -> 439 us
  local copies, waits for them, and re-layouts: 290 us -> 304 us
    all_to_all x0 -> x1, waiting for transfers between devices: none -> 221 us  [gather_by_exchange(): lax.all_to_all(jnp.tile(array, repeats), axis, split_axis=dim, concat_axi...]
    all_gather x1 -> x0, waiting for transfers between devices: 112 us -> none  [per_device(): lax.all_gather(in_weight, 'seq', axis=1, tiled=True)]
    another operation x0 -> x1, local copies, waits for them, and re-layouts: none -> 14.3 us  [gather_by_exchange(): jnp.tile(array, repeats)]
  transfers between devices with their start and end apart: 24 -> 24, of which waited for: 23 -> 23; matrix products, arithmetic and copies ran while one was open for 43% -> 37% of each run, Pallas kernels for 0% -> 0%
where the time goes in v1:
time: 1070 us; the launch traced here: 1040 us
  waiting for transfers between devices  439 us (41%)
  local copies, waits for them, and re-layouts  304 us (28%)
  other arithmetic  109 us (10%)
  starting transfers between devices  99.7 us (9%)
  matrix products  47.6 us (4%)
  blocking collectives  30.1 us (3%)
  between operations  15.4 us (1%)
    pad x24, local copies, waits for them, and re-layouts, per_device(): lax.associative_scan(combine_states, (decay, source), axis=0)  266 us
    all_to_all x1, waiting for transfers between devices, gather_by_exchange(): lax.all_to_all(jnp.tile(array, repeats), axis, split_axis=dim, concat_axi...  221 us
    ppermute x16, starting transfers between devices, from_behind(): return lax.ppermute(block, axis, route)  84.1 us
    psum x1, waiting for transfers between devices, per_device(): lax.psum(partial_value[:, :RANK].astype(jnp.bfloat16), 'expert')  47.5 us
    reduce_scatter x1, waiting for transfers between devices, per_device(): lax.psum_scatter(terms.astype(jnp.bfloat16), 'expert', scatter_dimension=...  39.9 us
    reduce_scatter x1, waiting for transfers between devices, per_device(): lax.psum_scatter(jnp.dot(act, w_down[0], preferred_element_type=jnp.float...  38 us
    add x12, other arithmetic, combine_states(): return (earlier[0] * later[0], later[0] * earlier[1] + later[1])  34.3 us
    add x12, other arithmetic, per_device(): lax.associative_scan(combine_states, (decay, source), axis=0)  33.2 us
  transfers between devices with their start and end apart: 24, of which 23 were waited for; matrix products, arithmetic and copies ran while one was open for 37% of the time, Pallas kernels for 0%

profile of v1, /device:TPU:0, one launch (start us, length us, event | category | flops | bytes accessed | tf_op | source)
XLA Modules:
  0.0 1044.9 jit_solution(4513967635986019718)
XLA Ops:
  9.7 14.3 %tile.4 = bf16[2,16,256,1024]{3,0,2,1:T(2,128)(2,1)} broadcast(bf16[2,256,1024]{2,0,1:T(2,128)(2,1)S(1)} %copy.46), dimensions={0,2,3} | broadcast | bytes 17825792 | tf_op jit(solution)/shard_map/tile | solution.py:16
  24.0 8.3 all-to-all-start
  33.2 26.6 %all-gather.4.cloned.1.call-done = bf16[128,4096]{1,0:T(8,128)(2,1)} async-done(((bf16[16,4096]{1,0:T(8,128)(2,1)}), bf16[128,4096]{1,0:T(8,128)(2,1)}) %all-gather.4.cloned.1.call-update) | async-done | bytes 1048592 | tf_op jit(solution)/shard_map/all_gather | solution.py:57
  61.3 220.8 %all-to-all-done = bf16[2,4096,1024]{2,0,1:T(2,128)(2,1)} async-done(((bf16[2,4096,1024]{2,0,1:T(2,128)(2,1)}), bf16[2,4096,1024]{2,0,1:T(2,128)(2,1)}, u32[]{:S(2)}, u32[]{:S(2)}) %all-to-all-start) | async-done | bytes 16777248 | tf_op jit(solution)/shard_map/all_to_all | solution.py:15
  282.1 11.2 %fusion.2 = f32[128,2,1024]{2,0,1:T(8,128)S(1)} fusion(bf16[2,4096,1024]{2,0,1:T(2,128)(2,1)} %all-to-all-done, bf16[128,4096]{1,0:T(8,128)(2,1)} %all-gather.4.cloned.1.call-done, f32[4096]{0:T(1024)S(1)} %copy-done.44, f32[128]{0:T(128)S(1)} %add_rsqrt_fusion.1), kind=kOutput, calls=%fused_computation.3 | convolution fusion | flops 2149580800 | bytes 18891264 | tf_op jit(solution)/shard_map/td,kdc->tkc/dot_general | solution.py:60
  298.1 13.2 %psum.14 = bf16[128,32]{0,1:T(8,128)(2,1)S(1)} all-reduce(bf16[128,32]{0,1:T(8,128)(2,1)S(1)} %slice.341), channel_id=1, replica_groups=mesh['seq'=16,'expert'=8] {'expert'}, use_global_device_ids=true, to_apply=%region_1.2 | all-reduce | flops 4096 | bytes 16384 | tf_op jit(solution)/shard_map/psum | solution.py:77
  312.1 47.5 %all-reduce.30.cloned.1.call-done = bf16[128,256]{0,1:T(8,128)(2,1)} async-done(((bf16[128,256]{0,1:T(8,128)(2,1)}), bf16[128,256]{0,1:T(8,128)(2,1)}) %all-reduce.30.cloned.1.call-update) | async-done | bytes 65552 | tf_op jit(solution)/shard_map/psum | solution.py:76
  370.1 10.7 %slice_add_fusion = (f32[64,16,1024]{2,1,0:T(8,128)S(1)}, f32[64,16,1024]{2,1,0:T(8,128)}) fusion(f32[128,16,1024]{2,1,0:T(8,128)} %copy-done.3, f32[128,16,1024]{2,1,0:T(8,128)} %copy-done.2), kind=kLoop, calls=%fused_computation.21 | loop fusion | flops 3145728 | bytes 25165824 | tf_op jit(solution)/shard_map/add | solution.py:32
  444.6 7.0 pad.108
  451.6 10.2 pad.109
  461.7 10.1 pad.95
  474.1 10.1 pad.94
  484.3 4.3 add.255
  491.5 5.0 fusion.18
  498.1 18.6 %pad.96 = f32[64,16,1024]{2,1,0:T(8,128)} pad(f32[32,16,1024]{2,1,0:T(8,128)} %pad_maximum_fusion.2, f32[]{:T(128)} %constant.11.clone.1), padding=0_1_1x0_0_0x0_0_0 | pad | bytes 6291460 | tf_op jit(solution)/shard_map/pad | solution.py:86
  516.7 11.9 %pad.97 = f32[64,16,1024]{2,1,0:T(8,128)} pad(f32[32,16,1024]{2,1,0:T(8,128)S(1)} %copy-done.16, f32[]{:T(128)} %constant.11.clone.1), padding=1_0_1x0_0_0x0_0_0 | pad | bytes 6291460 | tf_op jit(solution)/shard_map/pad | solution.py:86
  528.7 6.9 add.257
  535.5 35.6 %pad.99 = f32[128,16,1024]{2,1,0:T(8,128)} pad(f32[64,16,1024]{2,1,0:T(8,128)} %add.257, f32[]{:T(128)} %constant.11.clone.1), padding=1_0_1x0_0_0x0_0_0 | pad | bytes 12582916 | tf_op jit(solution)/shard_map/pad | solution.py:86
  572.5 18.6 %pad.110 = f32[64,16,1024]{2,1,0:T(8,128)} pad(f32[32,16,1024]{2,1,0:T(8,128)} %pad_maximum_fusion.3, f32[]{:T(128)} %constant.11.clone.1), padding=0_1_1x0_0_0x0_0_0 | pad | bytes 6291460 | tf_op jit(solution)/shard_map/pad | solution.py:86
  591.1 12.1 %pad.111 = f32[64,16,1024]{2,1,0:T(8,128)} pad(f32[32,16,1024]{2,1,0:T(8,128)S(1)} %copy-done.15, f32[]{:T(128)} %constant.11.clone.1), padding=1_0_1x0_0_0x0_0_0 | pad | bytes 6291460 | tf_op jit(solution)/shard_map/pad | solution.py:86
  603.3 7.1 add.265
  611.9 7.6 fusion.14
  621.9 35.5 %pad.98 = f32[128,16,1024]{2,1,0:T(8,128)} pad(f32[64,16,1024]{2,1,0:T(8,128)} %pad_maximum_fusion, f32[]{:T(128)} %constant.11.clone.1), padding=0_1_1x0_0_0x0_0_0 | pad | bytes 12582916 | tf_op jit(solution)/shard_map/pad | solution.py:86
  657.4 35.6 %pad.113 = f32[128,16,1024]{2,1,0:T(8,128)} pad(f32[64,16,1024]{2,1,0:T(8,128)} %add.265, f32[]{:T(128)} %constant.11.clone.1), padding=1_0_1x0_0_0x0_0_0 | pad | bytes 12582916 | tf_op jit(solution)/shard_map/pad | solution.py:86
  693.0 4.8 pad_maximum_fusion.1
  697.8 35.5 %pad.112 = f32[128,16,1024]{2,1,0:T(8,128)} pad(f32[64,16,1024]{2,1,0:T(8,128)} %pad_maximum_fusion.1, f32[]{:T(128)} %constant.11.clone.1), padding=0_1_1x0_0_0x0_0_0 | pad | bytes 12582916 | tf_op jit(solution)/shard_map/pad | solution.py:86
  735.1 107.0 %while.11 = (s32[]{:T(128)}, f32[16,1024]{1,0:T(8,128)S(1)}, f32[16,1024]{1,0:T(8,128)S(1)}, f32[16,1024]{1,0:T(8,128)S(1)}, s32[]{:T(128)}, /*index=5*/s32[]{:T(128)}) while((s32[]{:T(128)}, f32[16,1024]{1,0:T(8,128)S(1)}, f32[16,1024]{1,0:T(8,128)S(1)}, f32[16,1024]{1,0:T(8,128)S(1)}, s32[]{:T(128)}, /*index=5*/s32[]{:T(128)}) %tuple.47), condition=%wide.region_4.5_spmd.clone, body=%wide.region_3.4_spmd.clone.sunk | while | flops 81923 | bytes 458871 | solution.py:95
  745.9 4.4 collective-permute-start
  763.6 5.2 collective-permute-start
  770.3 6.3 collective-permute-start
  778.3 6.4 collective-permute-start
  786.3 6.3 collective-permute-start
  794.3 6.3 collective-permute-start
  802.2 6.3 collective-permute-start
  810.3 6.2 collective-permute-start
  818.1 6.3 collective-permute-start
  826.0 6.5 collective-permute-start
  834.2 6.3 collective-permute-start
  842.1 14.0 %multiply_reduce_fusion = f32[128,1024]{1,0:T(8,128)S(1)} fusion(f32[128,16,1024]{2,1,0:T(8,128)} %pad.112, f32[128,16,1024]{2,1,0:T(8,128)} %pad.113, f32[128,16,1024]{2,1,0:T(8,128)} %pad.98, f32[128,16,1024]{2,1,0:T(8,128)} %pad.99, f32[16,1024]{1,0:T(8,128)S(1)} %get-tuple-element.27, f32[128,16]{1,0:T(8,128)S(1)} %copy-done.28), kind=kLoop, calls=%fused_computation.5 | loop fusion | flops 12451840 | bytes 34152448 | tf_op jit(solution)/shard_map/reduce_sum | solution.py:97
  856.2 5.7 convolution_convert_fusion
  862.6 39.9 %reduce-scatter.3.cloned.1.call-done = bf16[16,4096]{1,0:T(8,128)(2,1)} async-done(((bf16[128,4096]{1,0:T(8,128)(2,1)}), bf16[16,4096]{1,0:T(8,128)(2,1)}) %reduce-scatter.3.cloned.1.call-update) | async-done | bytes 131088 | tf_op jit(solution)/shard_map/reduce_scatter | solution.py:104
  905.0 16.9 %all_to_all.15 = bf16[16,4,4096]{2,1,0:T(4,128)(2,1)S(1)} all-to-all(bf16[16,4,4096]{2,1,0:T(4,128)(2,1)S(1)} %reshape.83), channel_id=1, replica_groups=mesh['seq'=16,'expert'=8] {'seq'}, dimensions={0} | all-to-all | bytes 1048576 | tf_op jit(solution)/shard_map/all_to_all | solution.py:121
  923.0 29.3 %all-gather.8.cloned.1.call-done = bf16[8,64,4096]{2,1,0:T(8,128)(2,1)} async-done(((bf16[1,64,4096]{2,1,0:T(8,128)(2,1)}), bf16[8,64,4096]{2,1,0:T(8,128)(2,1)}) %all-gather.8.cloned.1.call-update) | async-done | bytes 4194320 | tf_op jit(solution)/shard_map/all_gather | solution.py:124
  952.3 10.1 fusion.8
  962.3 16.8 %fusion.10 = bf16[512,4096]{1,0:T(8,128)(2,1)} fusion(bf16[1,896,4096]{2,1,0:T(8,128)(2,1)} %param.35, f32[512,896]{1,0:T(8,128)} %fusion.8, bf16[512,4096]{1,0:T(8,128)(2,1)} %bitcast.53, bf16[1,4096,896]{2,1,0:T(8,128)(2,1)} %param.34), kind=kOutput, calls=%fused_computation.13 | convolution fusion | flops 7521042432 | bytes 24903680 | tf_op jit(solution)/shard_map/dot_general | solution.py:131
  979.2 38.0 %reduce-scatter.5.cloned.1.call-done = bf16[64,4096]{1,0:T(8,128)(2,1)} async-done(((bf16[512,4096]{1,0:T(8,128)(2,1)}), bf16[64,4096]{1,0:T(8,128)(2,1)}) %reduce-scatter.5.cloned.1.call-update) | async-done | bytes 524304 | tf_op jit(solution)/shard_map/reduce_scatter | solution.py:130
  1019.2 7.1 all-to-all-start.2
  1026.4 10.1 all-to-all-done.2
  (244 shorter events, 146.0 us)
Async XLA Ops:
  7.4 289.1 %copy-start = (bf16[1024,288]{0,1:T(8,128)(2,1)S(1)}, bf16[1024,288]{0,1:T(8,128)(2,1)}, u32[]{:S(2)}) copy-start(bf16[1024,288]{0,1:T(8,128)(2,1)} %param.24) | copy-start | bytes 1769476
  24.0 9.1 copy-start.39
  24.0 258.0 %copy-start.44 = (f32[4096]{0:T(1024)S(1)}, f32[4096]{0:T(1024)}, u32[]{:S(2)}) copy-start(f32[4096]{0:T(1024)} %param.20) | copy-start | bytes 49156
  24.0 258.0 %all-to-all-start = ((bf16[2,4096,1024]{2,0,1:T(2,128)(2,1)}), bf16[2,4096,1024]{2,0,1:T(2,128)(2,1)}, u32[]{:S(2)}, u32[]{:S(2)}) async-start(bf16[2,4096,1024]{2,0,1:T(2,128)(2,1)} %bitcast.47), calls=%async_computation | async-start | bytes 33554432 | tf_op jit(solution)/shard_map/all_to_all | solution.py:15
  32.3 27.4 %all-gather.4.cloned.1.call-start = ((), (), s32[]{:S(2)}) async-start(), calls=%async_computation.5 | async-start | bytes 1179648 | tf_op jit(solution)/shard_map/all_gather | solution.py:57
  33.1 326.6 %all-reduce.30.cloned.1.call-start = ((), (), s32[]{:S(2)}) async-start(), calls=%async_computation.6 | async-start | bytes 131072 | tf_op jit(solution)/shard_map/psum | solution.py:76
  61.3 234.9 %copy-start.40 = (f32[1024]{0:T(1024)S(1)}, f32[1024]{0:T(1024)}, u32[]{:S(2)}) copy-start(f32[1024]{0:T(1024)} %param.23) | copy-start | bytes 12292
  61.3 298.4 %copy-start.43 = (bf16[256,1024]{1,0:T(8,128)(2,1)S(1)}, bf16[256,1024]{1,0:T(8,128)(2,1)}, u32[]{:S(2)}) copy-start(bf16[256,1024]{1,0:T(8,128)(2,1)} %param.25) | copy-start | bytes 1572868
  61.3 298.4 %copy-start.45 = (f32[1024]{0:T(1024)S(1)}, f32[1024]{0:T(1024)}, u32[]{:S(2)}) copy-start(f32[1024]{0:T(1024)} %param.26) | copy-start | bytes 12292
  293.2 67.8 %copy-start.37 = (f32[16,1024]{1,0:T(8,128)S(1)}, f32[16,1024]{1,0:T(8,128)}, u32[]{:S(2)}) copy-start(f32[16,1024]{1,0:T(8,128)} %param.27) | copy-start | bytes 196612
  293.3 2.9 collective-permute-start.1
  296.5 66.9 %copy-start.21 = (bf16[128,1024]{1,0:T(8,128)(2,1)}, bf16[128,1024]{1,0:T(8,128)(2,1)S(1)}, u32[]{:S(2)}) copy-start(bf16[128,1024]{1,0:T(8,128)(2,1)S(1)} %multiply_convert_fusion.1) | copy-start | bytes 786436
  297.5 558.6 %all-gather.6.cloned.1.call-start = ((), (), s32[]{:S(2)}) async-start(), calls=%async_computation.7 | async-start | bytes 8912896 | tf_op jit(solution)/shard_map/all_gather | solution.py:101
  298.1 604.4 %reduce-scatter.3.cloned.1.call-start = ((), (), s32[]{:S(2)}) async-start(), calls=%async_computation.8 | async-start | bytes 1179648 | tf_op jit(solution)/shard_map/reduce_scatter | solution.py:104
  444.6 27.2 %copy-start.33 = (f32[1,16,1024]{2,1,0:T(8,128)S(1)}, f32[1,16,1024]{2,1,0:T(8,128)}, u32[]{:S(2)}) copy-start(f32[1,16,1024]{2,1,0:T(8,128)} %slice.347) | copy-start | bytes 196612
  498.1 18.6 %copy-start.16 = (f32[32,16,1024]{2,1,0:T(8,128)S(1)}, f32[32,16,1024]{2,1,0:T(8,128)}, u32[]{:S(2)}) copy-start(f32[32,16,1024]{2,1,0:T(8,128)} %add.255) | copy-start | bytes 6291460
  535.5 35.6 %copy-start.17 = (f32[31,16,1024]{2,1,0:T(8,128)S(1)}, f32[31,16,1024]{2,1,0:T(8,128)}, u32[]{:S(2)}) copy-start(f32[31,16,1024]{2,1,0:T(8,128)} %get-tuple-element.56) | copy-start | bytes 6094852
  535.5 35.6 %copy-start.31 = (f32[1,16,1024]{2,1,0:T(8,128)S(1)}, f32[1,16,1024]{2,1,0:T(8,128)}, u32[]{:S(2)}) copy-start(f32[1,16,1024]{2,1,0:T(8,128)} %slice.369) | copy-start | bytes 196612
  572.5 18.6 %copy-start.15 = (f32[32,16,1024]{2,1,0:T(8,128)S(1)}, f32[32,16,1024]{2,1,0:T(8,128)}, u32[]{:S(2)}) copy-start(f32[32,16,1024]{2,1,0:T(8,128)} %add.264) | copy-start | bytes 6291460
  603.2 8.6 copy-start.6
  657.4 35.6 %copy-start.29 = (f32[1,16,1024]{2,1,0:T(8,128)S(1)}, f32[1,16,1024]{2,1,0:T(8,128)}, u32[]{:S(2)}) copy-start(f32[1,16,1024]{2,1,0:T(8,128)} %slice.368) | copy-start | bytes 196612
  697.8 144.3 %copy-start.28 = (f32[128,16]{1,0:T(8,128)S(1)}, f32[128,16]{1,0:T(8,128)}, u32[]{:S(2)}) copy-start(f32[128,16]{1,0:T(8,128)} %copy.48) | copy-start | bytes 24580
  735.1 4.9 collective-permute-start
  740.0 5.9 collective-permute-start
  745.9 6.0 collective-permute-start
  751.9 5.8 collective-permute-start
  757.7 5.8 collective-permute-start
  763.6 6.8 collective-permute-start
  770.3 7.9 collective-permute-start
  778.3 8.0 collective-permute-start
  786.3 7.9 collective-permute-start
  794.3 7.9 collective-permute-start
  802.2 8.0 collective-permute-start
  810.3 7.8 collective-permute-start
  818.1 7.9 collective-permute-start
  826.0 8.1 collective-permute-start
  834.2 7.9 collective-permute-start
  842.1 14.1 %copy-start.22 = (bf16[128,1024]{1,0:T(8,128)(2,1)S(1)}, bf16[128,1024]{1,0:T(8,128)(2,1)}, u32[]{:S(2)}) copy-start(bf16[128,1024]{1,0:T(8,128)(2,1)} %copy-done.21) | copy-start | bytes 786436
  842.1 14.1 %copy-start.27 = (f32[128,2,1024]{2,0,1:T(8,128)S(1)}, f32[128,2,1024]{2,0,1:T(8,128)}, u32[]{:S(2)}) copy-start(f32[128,2,1024]{2,0,1:T(8,128)} %copy-done.26) | copy-start | bytes 3145732
  842.1 14.1 %copy-start.46 = (f32[1024]{0:T(1024)S(1)}, f32[1024]{0:T(1024)}, u32[]{:S(2)}) copy-start(f32[1024]{0:T(1024)} %param.28) | copy-start | bytes 12292
  856.1 46.4 %copy-start.19 = (bf16[16,4096]{1,0:T(8,128)(2,1)S(1)}, bf16[16,4096]{1,0:T(8,128)(2,1)}, u32[]{:S(2)}) copy-start(bf16[16,4096]{1,0:T(8,128)(2,1)} %param.19) | copy-start | bytes 393220
  856.1 47.5 %copy-start.38 = (f32[4096]{0:T(1024)S(1)}, f32[4096]{0:T(1024)}, u32[]{:S(2)}) copy-start(f32[4096]{0:T(1024)} %param.30) | copy-start | bytes 49156
  861.9 90.4 %all-gather.8.cloned.1.call-start = ((), (), s32[]{:S(2)}) async-start(), calls=%async_computation.9 | async-start | bytes 4718592 | tf_op jit(solution)/shard_map/all_gather | solution.py:124
  922.9 94.3 %reduce-scatter.5.cloned.1.call-start = ((), (), s32[]{:S(2)}) async-start(), calls=%async_computation.10 | async-start | bytes 4718592 | tf_op jit(solution)/shard_map/reduce_scatter | solution.py:130
  962.3 75.2 %copy-start.1 = (bf16[1024,288]{0,1:T(8,128)(2,1)S(1)}, bf16[1024,288]{0,1:T(8,128)(2,1)}, u32[]{:S(2)}) copy-start(bf16[1024,288]{0,1:T(8,128)(2,1)} %param.24) | copy-start | bytes 1769476
  979.1 47.2 %copy-start.42 = (f32[16,2]{0,1:T(2,128)S(1)}, f32[16,2]{0,1:T(2,128)}, u32[]{:S(2)}) copy-start(f32[16,2]{0,1:T(2,128)} %param.32) | copy-start | bytes 388
  979.1 57.4 %copy-start.20 = (bf16[16,4096]{1,0:T(8,128)(2,1)S(1)}, bf16[16,4096]{1,0:T(8,128)(2,1)}, u32[]{:S(2)}) copy-start(bf16[16,4096]{1,0:T(8,128)(2,1)} %reduce-scatter.3.cloned.1.call-done) | copy-start | bytes 393220
  1019.2 17.2 %all-to-all-start.2 = ((bf16[16,4,4096]{2,1,0:T(4,128)(2,1)}), bf16[16,4,4096]{2,1,0:T(4,128)(2,1)S(1)}, u32[]{:S(2)}, u32[]{:S(2)}) async-start(bf16[16,4,4096]{2,1,0:T(4,128)(2,1)} %reshape.86), calls=%async_computation.4 | async-start | bytes 1048576 | tf_op jit(solution)/shard_map/all_to_all | solution.py:136
  (23 other events, 102.9 us)
Sparse Core Ops, SparseCore 0:
  34.9 24.8 all-gather.3
  297.6 62.0 all-reduce.29
  862.0 40.4 reduce-scatter.2
  923.0 29.1 all-gather.7
  979.3 37.8 reduce-scatter.4
Sparse Core Ops, SparseCore 1:
  300.3 79.9 all-gather.5
